TPU v7x, 32 devices: a whole 2x2x4 slice. The times are simulated.
32 devices in a mesh: dp: 16 (over z, x, core), mp: 2 (over y).
Axes of the slice: x: 2, y: 2, z: 4, core: 2. Of those that a mesh axis runs over, the one named last changes fastest.
Arguments:
- x_in: bfloat16 [128, 1024, 512], P('dp', 'mp'), may hold values from -6 to 6
- d_in: bfloat16 [128, 1024, 512], P('dp', 'mp'), may hold values from -6 to 6
- segments: int32 [128, 1024], P('dp'), may hold values from 0 to 65, as said below
- cot_x: bfloat16 [128, 1024, 512], P('dp', 'mp'), may hold values from -6 to 6
- cot_d: bfloat16 [128, 1024, 512], P('dp', 'mp'), may hold values from -6 to 6
- w_qkv: float32 [512, 3, 512], P('dp', None, 'mp'), may hold values from -0.25 to 0.25
- w_out: float32 [512, 512], P('mp', 'dp'), may hold values from -2 to 2
- w_in: float32 [512, 2048], P('dp', 'mp'), may hold values from -0.25 to 0.25
- w_back: float32 [2048, 512], P('mp', 'dp'), may hold values from -0.125 to 0.125
- norms: float32 [4, 512], P(None, 'dp'), as said below
- qkv_mom: float32 [512, 3, 512], P('dp', None, 'mp'), may hold values from -4096 to 4096
- qkv_sec: float32 [512, 3, 512], P('dp', None, 'mp'), may hold values from 524288 to 2097152
- out_mom: float32 [512, 512], P('mp', 'dp'), may hold values from -640 to 640
- out_sec: float32 [512, 512], P('mp', 'dp'), may hold values from 11796.48 to 47185.92
- in_mom: float32 [512, 2048], P('dp', 'mp'), may hold values from -896 to 896
- in_sec: float32 [512, 2048], P('dp', 'mp'), may hold values from 20971.52 to 83886.08
- back_mom: float32 [2048, 512], P('mp', 'dp'), may hold values from -2048 to 2048
- back_sec: float32 [2048, 512], P('mp', 'dp'), may hold values from 131072 to 524288
- norm_mom: float32 [4, 512], P(None, 'dp'), may hold values from -3072 to 3072
- norm_sec: float32 [4, 512], P(None, 'dp'), may hold values from 294912 to 1179648
Outputs:
- x_out: bfloat16 [128, 1024, 512], P('dp', 'mp')
- d_out: bfloat16 [128, 1024, 512], P('dp', 'mp')
- x_grad: float32 [128, 1024, 512], P('dp', 'mp')
- qkv_mom_new: float32 [512, 3, 512], P('dp', None, 'mp')
- qkv_sec_new: float32 [512, 3, 512], P('dp', None, 'mp')
- qkv_new: float32 [512, 3, 512], P('dp', None, 'mp')
- out_mom_new: float32 [512, 512], P('mp', 'dp')
- out_sec_new: float32 [512, 512], P('mp', 'dp')
- out_new: float32 [512, 512], P('mp', 'dp')
- in_mom_new: float32 [512, 2048], P('dp', 'mp')
- in_sec_new: float32 [512, 2048], P('dp', 'mp')
- in_new: float32 [512, 2048], P('dp', 'mp')
- back_mom_new: float32 [2048, 512], P('mp', 'dp')
- back_sec_new: float32 [2048, 512], P('mp', 'dp')
- back_new: float32 [2048, 512], P('mp', 'dp')
- norm_mom_new: float32 [4, 512], P(None, 'dp')
- norm_sec_new: float32 [4, 512], P(None, 'dp')
- norm_new: float32 [4, 512], P(None, 'dp')
Inputs may be any that keep to these rules, and one draw needn't show every extreme that they name: `segments`: segment ids start at 0, never fall along a sequence, rise by at most one from a position to the next, and the last id of every sequence is exactly max(128, 2) // 2 + 1. `norms`: rows 0 and 2 are gains, rows 1 and 3 biases.
All inputs are finite; a program needn't handle non-finite values.
Results may differ from a plain program's by a relative error of at most 0.012.
The roundings to bfloat16 on the way count: a program that leaves them out, or rounds other values in their place, can miss the bound.
Values may be sent and summed in bfloat16 or wider, within the bound.
No kernel may reach another device: no remote copies, remote signals or barrier semaphores. Data moves between devices by JAX's collectives and lax.ppermute only.
A program may use at most 320 MiB of HBM per device.

v0:
```python
import jax
import jax.numpy as jnp
from jax import lax
from jax.sharding import PartitionSpec as P

STEP = 5
HD = 64


neg_fill = -1000000000.0
norm_eps = 1e-05
beta_first = 0.5
beta_second = 0.5
adam_eps = 1e-08
decay_rate = 0.01


def layer_norm(resid, gain_vals, bias_vals):
    center = resid - jnp.mean(resid, axis=-1, keepdims=True)
    spread = jnp.mean(center * center, axis=-1, keepdims=True)
    return center * lax.rsqrt(spread + norm_eps) * gain_vals + bias_vals


def gelu_exact(value):
    return jax.nn.gelu(value, approximate=False)


def visible(segment_ids):
    position = jnp.arange(segment_ids.shape[0])
    return (position[None, :] <= position[:, None]) & (segment_ids[None, :] == segment_ids[:, None])


def masked_scores(query_rows, key_rows, segment_ids):
    scale = query_rows.shape[-1] ** (-0.5)
    scores = (
        jnp.einsum("qhe,khe->hqk", query_rows, key_rows, preferred_element_type=jnp.float32) * scale
    )
    return (jnp.where(visible(segment_ids)[None], scores, neg_fill), scale)


def attend_forward(pieces):
    query_rows, key_rows, value_rows, segment_ids = pieces
    scores, scale = masked_scores(query_rows, key_rows, segment_ids)
    row_max = jnp.max(scores, axis=-1, keepdims=True)
    exponent = jnp.exp(scores - row_max)
    total = jnp.sum(exponent, axis=-1, keepdims=True)
    probabilities = (exponent / total).astype(jnp.bfloat16)
    mixture_rows = jnp.einsum(
        "hqk,khe->qhe", probabilities, value_rows, preferred_element_type=jnp.float32
    )
    return (mixture_rows.astype(jnp.bfloat16), (row_max + jnp.log(total))[..., 0])


def attend_backward(pieces):
    query_rows, key_rows, value_rows, grad_mixture, log_total, segment_ids = pieces
    scores, scale = masked_scores(query_rows, key_rows, segment_ids)
    probs_full = jnp.exp(scores - log_total[..., None])
    probabilities = probs_full.astype(jnp.bfloat16)
    grad_values = jnp.einsum(
        "hqk,qhe->khe", probabilities, grad_mixture, preferred_element_type=jnp.float32
    )
    grad_probs = jnp.einsum(
        "qhe,khe->hqk", grad_mixture, value_rows, preferred_element_type=jnp.float32
    )
    delta = jnp.sum(grad_probs * probs_full, axis=-1, keepdims=True)
    grad_scores = (probs_full * (grad_probs - delta)).astype(jnp.bfloat16)
    grad_queries = (
        jnp.einsum("hqk,khe->qhe", grad_scores, key_rows, preferred_element_type=jnp.float32)
        * scale
    )
    grad_keys = (
        jnp.einsum("hqk,qhe->khe", grad_scores, query_rows, preferred_element_type=jnp.float32)
        * scale
    )
    return (
        grad_queries.astype(jnp.bfloat16),
        grad_keys.astype(jnp.bfloat16),
        grad_values.astype(jnp.bfloat16),
    )


def layer_core(
    x_rows,
    d_rows,
    cot_x_rows,
    cot_d_rows,
    segment_ids,
    query_key_value_matrix,
    output_matrix,
    input_matrix,
    backproj_matrix,
    gain_rows,
    handlers,
):
    (
        gather_stream,
        sum_attention,
        gather_normed,
        sum_feed,
        gather_feed,
        sum_normed,
        gather_branch,
        sum_input,
    ) = handlers
    whole_input_rows = gather_stream(x_rows)
    seq_count, length = (whole_input_rows.shape[0], whole_input_rows.shape[1])
    local_width = query_key_value_matrix.shape[2]
    head_count = local_width // HD
    projected_rows = jnp.einsum(
        "xor,rnq->xonq",
        whole_input_rows,
        query_key_value_matrix,
        preferred_element_type=jnp.float32,
    ).astype(jnp.bfloat16)
    shaped = projected_rows.reshape(seq_count, length, 3, head_count, HD)
    query_rows, key_rows, value_rows = (shaped[:, :, 0], shaped[:, :, 1], shaped[:, :, 2])
    mixture_rows, log_total = lax.map(
        attend_forward, (query_rows, key_rows, value_rows, segment_ids)
    )
    flattened_mixture = mixture_rows.reshape(seq_count, length, local_width)
    attended_rows = sum_attention(
        jnp.einsum(
            "mbi,iy->mby", flattened_mixture, output_matrix, preferred_element_type=jnp.float32
        )
    )
    first_input, norm_one_back = jax.vjp(
        layer_norm, x_rows.astype(jnp.float32) + attended_rows, gain_rows[0], gain_rows[1]
    )
    d_one = d_rows.astype(jnp.float32) + attended_rows
    whole_input_rows1 = gather_normed(first_input.astype(jnp.bfloat16))
    hidden_input = jnp.einsum(
        "eot,tv->eov", whole_input_rows1, input_matrix, preferred_element_type=jnp.float32
    )
    active_values, gelu_back = jax.vjp(gelu_exact, hidden_input)
    active_backward = active_values.astype(jnp.bfloat16)
    feedforward_output = sum_feed(
        jnp.einsum(
            "mbi,iy->mby", active_backward, backproj_matrix, preferred_element_type=jnp.float32
        )
    )
    x_two, norm_two_back = jax.vjp(
        layer_norm, first_input + feedforward_output, gain_rows[2], gain_rows[3]
    )
    d_two = d_one + feedforward_output
    carry_dual = cot_d_rows.astype(jnp.float32)
    grad_r2, grad_g2, grad_b2 = norm_two_back(cot_x_rows.astype(jnp.float32))
    grad_feed = (grad_r2 + carry_dual).astype(jnp.bfloat16)
    whole_forward_gradient = gather_feed(grad_feed)
    grad_active = jnp.einsum(
        "wqo,uo->wqu", whole_forward_gradient, backproj_matrix, preferred_element_type=jnp.float32
    )
    hidden_gradient = gelu_back(grad_active)[0].astype(jnp.bfloat16)
    backproj_gradient = jnp.einsum(
        "ovx,ovu->xu", active_backward, whole_forward_gradient, preferred_element_type=jnp.float32
    )
    input_gradient = jnp.einsum(
        "upj,upv->jv", whole_input_rows1, hidden_gradient, preferred_element_type=jnp.float32
    )
    grad_x1 = grad_r2 + sum_normed(
        jnp.einsum("ipw,gw->ipg", hidden_gradient, input_matrix, preferred_element_type=jnp.float32)
    )
    grad_r1, grad_g1, grad_b1 = norm_one_back(grad_x1)
    grad_branch = (grad_r1 + carry_dual).astype(jnp.bfloat16)
    whole_backward_gradient = gather_branch(grad_branch)
    grad_mixture = jnp.einsum(
        "wqo,uo->wqu", whole_backward_gradient, output_matrix, preferred_element_type=jnp.float32
    ).astype(jnp.bfloat16)
    output_gradient = jnp.einsum(
        "ovx,ovu->xu",
        flattened_mixture,
        whole_backward_gradient,
        preferred_element_type=jnp.float32,
    )
    grad_queries, grad_keys, grad_values = lax.map(
        attend_backward,
        (
            query_rows,
            key_rows,
            value_rows,
            grad_mixture.reshape(seq_count, length, head_count, HD),
            log_total,
            segment_ids,
        ),
    )
    projected_gradient = jnp.stack([grad_queries, grad_keys, grad_values], axis=2).reshape(
        seq_count, length, 3, local_width
    )
    qkv_grad = jnp.einsum(
        "emn,emjo->njo", whole_input_rows, projected_gradient, preferred_element_type=jnp.float32
    )
    norm_local = jnp.stack([grad_g1, grad_b1, grad_g2, grad_b2])
    input_part, norm_grad = sum_input(
        jnp.einsum(
            "uzvt,ivt->uzi",
            projected_gradient,
            query_key_value_matrix,
            preferred_element_type=jnp.float32,
        ),
        norm_local,
    )
    grad_x = grad_r1 + input_part
    return (
        x_two.astype(jnp.bfloat16),
        d_two.astype(jnp.bfloat16),
        grad_x,
        (qkv_grad, output_gradient, input_gradient, backproj_gradient),
        norm_grad,
    )


def adam_update(weight, grad, mom, sec, rate):
    mom_new = beta_first * mom + (1.0 - beta_first) * grad
    sec_new = beta_second * sec + (1.0 - beta_second) * grad * grad
    scaled = (
        mom_new
        / (1.0 - beta_first**STEP)
        / (jnp.sqrt(sec_new / (1.0 - beta_second**STEP)) + adam_eps)
    )
    return (mom_new, sec_new, weight - rate * (scaled + decay_rate * weight))


def on_device(
    x_in,
    d_in,
    segments,
    cot_x,
    cot_d,
    w_qkv,
    w_out,
    w_in,
    w_back,
    norms,
    qkv_mom,
    qkv_sec,
    out_mom,
    out_sec,
    in_mom,
    in_sec,
    back_mom,
    back_sec,
    norm_mom,
    norm_sec,
):
    half = jnp.bfloat16
    query_key_value_matrix, output_matrix, input_matrix, backproj_matrix, gain_copy = (
        lax.all_gather(w_qkv.astype(half), "dp", axis=0, tiled=True),
        lax.all_gather(w_out.astype(half), "dp", axis=1, tiled=True),
        lax.all_gather(w_in.astype(half), "dp", axis=0, tiled=True),
        lax.all_gather(w_back.astype(half), "dp", axis=1, tiled=True),
        lax.all_gather(norms.astype(half), "dp", axis=1, tiled=True),
    )
    gain_rows = gain_copy.astype(jnp.float32)

    def gather_stream(value):
        return lax.all_gather(value, "mp", axis=1, tiled=True)

    def sum_attention(value):
        return lax.psum_scatter(value, "mp", scatter_dimension=1, tiled=True)

    def gather_normed(value):
        return lax.all_gather(value, "mp", axis=1, tiled=True)

    def sum_feed(value):
        return lax.psum_scatter(value, "mp", scatter_dimension=1, tiled=True)

    def gather_feed(value):
        return lax.all_gather(value, "mp", axis=1, tiled=True)

    def sum_normed(value):
        return lax.psum_scatter(value, "mp", scatter_dimension=1, tiled=True)

    def gather_branch(value):
        return lax.all_gather(value, "mp", axis=1, tiled=True)

    def sum_input(value, norm_local):
        norm_tiled = jnp.tile(norm_local, (lax.axis_size("mp"), 1))
        return (
            lax.psum_scatter(value, "mp", scatter_dimension=1, tiled=True),
            lax.psum_scatter(norm_tiled, "mp", scatter_dimension=0, tiled=True),
        )

    handlers = (
        gather_stream,
        sum_attention,
        gather_normed,
        sum_feed,
        gather_feed,
        sum_normed,
        gather_branch,
        sum_input,
    )
    x_out, d_out, x_grad, grads, norm_grad = layer_core(
        x_in,
        d_in,
        cot_x,
        cot_d,
        segments,
        query_key_value_matrix,
        output_matrix,
        input_matrix,
        backproj_matrix,
        gain_rows,
        handlers,
    )
    qkv_g, out_g, in_g, back_g, norm_g = (
        lax.psum_scatter(grads[0], "dp", scatter_dimension=0, tiled=True),
        lax.psum_scatter(grads[1], "dp", scatter_dimension=1, tiled=True),
        lax.psum_scatter(grads[2], "dp", scatter_dimension=0, tiled=True),
        lax.psum_scatter(grads[3], "dp", scatter_dimension=1, tiled=True),
        lax.psum_scatter(norm_grad, "dp", scatter_dimension=1, tiled=True),
    )
    qkv_state = adam_update(w_qkv, qkv_g, qkv_mom, qkv_sec, 0.05)
    out_state = adam_update(w_out, out_g, out_mom, out_sec, 0.3)
    in_state = adam_update(w_in, in_g, in_mom, in_sec, 0.05)
    back_state = adam_update(w_back, back_g, back_mom, back_sec, 0.025)
    norm_state = adam_update(norms, norm_g, norm_mom, norm_sec, 0.1)
    return (
        x_out,
        d_out,
        x_grad,
        qkv_state[0],
        qkv_state[1],
        qkv_state[2],
        out_state[0],
        out_state[1],
        out_state[2],
        in_state[0],
        in_state[1],
        in_state[2],
        back_state[0],
        back_state[1],
        back_state[2],
        norm_state[0],
        norm_state[1],
        norm_state[2],
    )


def solution(mesh):
    return jax.shard_map(
        on_device,
        mesh=mesh,
        in_specs=(
            P("dp", "mp", None),
            P("dp", "mp", None),
            P("dp", None),
            P("dp", "mp", None),
            P("dp", "mp", None),
            P("dp", None, "mp"),
            P("mp", "dp"),
            P("dp", "mp"),
            P("mp", "dp"),
            P(None, "dp"),
            P("dp", None, "mp"),
            P("dp", None, "mp"),
            P("mp", "dp"),
            P("mp", "dp"),
            P("dp", "mp"),
            P("dp", "mp"),
            P("mp", "dp"),
            P("mp", "dp"),
            P(None, "dp"),
            P(None, "dp"),
        ),
        out_specs=(
            P("dp", "mp", None),
            P("dp", "mp", None),
            P("dp", "mp", None),
            P("dp", None, "mp"),
            P("dp", None, "mp"),
            P("dp", None, "mp"),
            P("mp", "dp"),
            P("mp", "dp"),
            P("mp", "dp"),
            P("dp", "mp"),
            P("dp", "mp"),
            P("dp", "mp"),
            P("mp", "dp"),
            P("mp", "dp"),
            P("mp", "dp"),
            P(None, "dp"),
            P(None, "dp"),
            P(None, "dp"),
        ),
        check_vma=False,
    )
```

profile of v0, /device:TPU:0, one launch (start us, length us, event | category | flops | bytes accessed | tf_op | source)
XLA Modules:
  0.0 2116.0 jit_solution(9568646862205261386)
XLA Ops:
  10.5 25.2 %all_gather.29 = bf16[256,512]{0,1:T(8,128)(2,1)} all-gather(bf16[256,32]{0,1:T(8,128)(2,1)S(1)} %convert_element_type.93), channel_id=1, replica_groups=mesh['dp'=16,'mp'=2] {'dp'}, dimensions={1}, use_global_device_ids=true | all-gather | bytes 278528 | tf_op jit(solution)/shard_map/all_gather | solution.py:247
  35.7 19.6 all_gather.28
  55.2 61.9 %all-gather.8.cloned.1.call-done = bf16[8,1024,512]{2,1,0:T(8,128)(2,1)} async-done(((bf16[8,512,512]{2,1,0:T(8,128)(2,1)}), bf16[8,1024,512]{2,1,0:T(8,128)(2,1)}) %all-gather.8.cloned.1.call-update) | async-done | bytes 8388624 | tf_op jit(solution)/shard_map/all_gather | solution.py:255
  117.1 13.0 fusion.74
  130.2 8.9 slice_bitcast_fusion
  141.5 134.3 %while.26 = (s32[]{:T(128)}, bf16[8,1024,4,64]{1,3,2,0:T(8,128)(2,1)}, f32[8,4,1024]{2,1,0:T(4,128)}, bf16[8,1024,4,64]{1,3,2,0:T(8,128)(2,1)}, s32[8,1024]{1,0:...) while((s32[]{:T(128)}, bf16[8,1024,4,64]{1,3,2,0:T(8,128)(2,1)}, ...), condition=%wide.region_3.4_spmd, body=%wide.region_0.3_spmd.sunk | while | flops 1127477248 | bytes 56769112 | solution.py:117
  275.8 10.3 fusion.95
  288.1 21.4 %all-gather = bf16[16,32,4]{1,2,0:T(4,128)(2,1)S(1)} all-gather(bf16[1,32,4]{1,2,0:T(4,128)(2,1)S(1)} %convert_bitcast_fusion), channel_id=1, replica_groups=mesh['dp'=16,'mp'=2] {'dp'}, dimensions={0}, use_global_device_ids=true | all-gather | bytes 4352 | tf_op jit(solution)/shard_map/all_gather | solution.py:250
  310.2 165.3 %reduce-scatter.11.cloned.1.call-done = f32[8,512,512]{2,1,0:T(8,128)} async-done(((f32[8,1024,512]{2,1,0:T(8,128)}), f32[8,512,512]{2,1,0:T(8,128)}) %reduce-scatter.11.cloned.1.call-update) | async-done | bytes 8388624 | tf_op jit(solution)/shard_map/reduce_scatter | solution.py:258
  487.9 103.2 %all-gather.10.cloned.1.call-done = bf16[8,1024,512]{2,1,0:T(8,128)(2,1)} async-done(((bf16[8,512,512]{2,1,0:T(8,128)(2,1)}), bf16[8,1024,512]{2,1,0:T(8,128)(2,1)}) %all-gather.10.cloned.1.call-update) | async-done | bytes 8388624 | tf_op jit(solution)/shard_map/all_gather | solution.py:261
  591.1 26.4 %fusion.73 = (u8[1024,1024]{1,0:T(8,128)(4,1)S(1)}, u8[1024,1024]{1,0:T(8,128)(4,1)S(1)}, f32[8,1024,1024]{2,1,0:T(8,128)}) fusion(bf16[8,1024,512]{2,1,0:T(8,128)(2,1)} %all-gather.10.cloned.1.call-done, bf16[512,1024]{1,0:T(8,128)(2,1)} %all-gather.12.cloned.1.call-done), kind=kOutput, calls=%fused_computation.113 | convolution fusion | flops 8696889344 | bytes 45088768 | tf_op jit(solution)/shard_map/eot,tv->eov/dot_general | solution.py:131
  617.5 77.2 %multiply_convert_fusion.1 = (bf16[8,1024,1024]{2,1,0:T(8,128)(2,1)}, f32[8,1024,1024]{2,1,0:T(8,128)}) fusion(f32[8,1024,1024]{2,1,0:T(8,128)} %get-tuple-element.252, u8[1024,1024]{1,0:T(8,128)(4,1)S(1)} %get-tuple-element.170, u8[1024,1024]{1,0:T(8,128)(4,1)S(1)} %get-tuple-element.169), kind=kLoop, calls=%fused_computation.72 | loop fusion | flops 587202560 | bytes 85983232 | tf_op jit(solution)/shard_map/convert_element_type | solution.py:135
  694.7 16.2 fusion.84
  711.0 189.2 %reduce-scatter.13.cloned.1.call-done = f32[8,512,512]{2,1,0:T(8,128)} async-done(((f32[8,1024,512]{2,1,0:T(8,128)}), f32[8,512,512]{2,1,0:T(8,128)}) %reduce-scatter.13.cloned.1.call-update) | async-done | bytes 8388624 | tf_op jit(solution)/shard_map/reduce_scatter | solution.py:264
  900.2 13.2 fusion.113
  929.1 104.1 %all-gather.16.cloned.1.call-done = bf16[8,1024,512]{2,1,0:T(8,128)(2,1)} async-done(((bf16[8,512,512]{2,1,0:T(8,128)(2,1)}), bf16[8,1024,512]{2,1,0:T(8,128)(2,1)}) %all-gather.16.cloned.1.call-update) | async-done | bytes 8388624 | tf_op jit(solution)/shard_map/all_gather | solution.py:267
  1033.2 32.1 %add_convert_fusion = bf16[8,1024,1024]{2,1,0:T(8,128)(2,1)} fusion(f32[8,1024,1024]{2,1,0:T(8,128)} %get-tuple-element.234, f32[8,1024,1024]{2,1,0:T(8,128)} %get-tuple-element.252, bf16[8,1024,512]{2,1,0:T(8,128)(2,1)} %all-gather.16.cloned.1.call-done, bf16[1024,512]{0,1:T(8,128)(2,1)S(1)} %copy-done.34), kind=kOutput, calls=%fused_computation.71 | convolution fusion | flops 8707375104 | bytes 93323264 | tf_op jit(solution)/shard_map/wqo,uo->wqu/dot_general | solution.py:149
  1065.3 15.8 fusion.88
  1081.1 189.1 %reduce-scatter.15.cloned.1.call-done = f32[8,512,512]{2,1,0:T(8,128)} async-done(((f32[8,1024,512]{2,1,0:T(8,128)}), f32[8,512,512]{2,1,0:T(8,128)}) %reduce-scatter.15.cloned.1.call-update) | async-done | bytes 8388624 | tf_op jit(solution)/shard_map/reduce_scatter | solution.py:270
  1270.2 15.3 multiply_reduce_fusion.1
  1297.5 16.4 convolution_bitcast_fusion.1
  1314.1 16.5 convolution_bitcast_fusion.2
  1340.5 61.5 %all-gather.18.cloned.1.call-done = bf16[8,1024,512]{2,1,0:T(8,128)(2,1)} async-done(((bf16[8,512,512]{2,1,0:T(8,128)(2,1)}), bf16[8,1024,512]{2,1,0:T(8,128)(2,1)}) %all-gather.18.cloned.1.call-update) | async-done | bytes 8388624 | tf_op jit(solution)/shard_map/all_gather | solution.py:273
  1402.0 7.7 convolution_convert_fusion
  1417.3 300.2 %while.27 = (s32[]{:T(128)}, bf16[8,1024,4,64]{1,3,2,0:T(8,128)(2,1)}, bf16[8,1024,4,64]{1,3,2,0:T(8,128)(2,1)}, bf16[8,1024,4,64]{1,3,2,0:T(8,128)(2,1)}, bf16[...) while((s32[]{:T(128)}, ...), condition=%wide.region_17.18_spmd, body=%wide.region_15.17_spmd.sunk | while | flops 2726555648 | bytes 133268592 | solution.py:174
  1425.3 9.4 multiply_reduce_fusion.6
  1434.7 7.9 multiply_convert_fusion.3
  1462.8 9.4 multiply_reduce_fusion.6
  1472.2 7.8 multiply_convert_fusion.3
  1500.4 9.4 multiply_reduce_fusion.6
  1509.8 7.8 multiply_convert_fusion.3
  1537.9 9.4 multiply_reduce_fusion.6
  1547.3 7.8 multiply_convert_fusion.3
  1575.4 9.4 multiply_reduce_fusion.6
  1584.8 7.8 multiply_convert_fusion.3
  1612.9 9.4 multiply_reduce_fusion.6
  1622.3 7.8 multiply_convert_fusion.3
  1650.3 9.4 multiply_reduce_fusion.6
  1659.8 7.8 multiply_convert_fusion.3
  1687.9 9.4 multiply_reduce_fusion.6
  1697.3 7.8 multiply_convert_fusion.3
  1736.8 12.4 fusion.79
  1751.1 8.9 convolution_bitcast_fusion.3
  1760.0 13.2 convolution_bitcast_fusion
  1780.0 68.9 %all-reduce.4.cloned.1.call-done = f32[512,3,256]{2,1,0:T(4,128)} async-done(((f32[512,3,256]{2,1,0:T(4,128)}), f32[512,3,256]{2,1,0:T(4,128)}) %all-reduce.4.cloned.1.call-update) | async-done | bytes 1572880
  1849.8 58.3 %reduce-scatter.19.cloned.1.call-done = f32[256,32]{0,1:T(8,128)} async-done(((f32[256,512]{0,1:T(8,128)}), f32[256,32]{0,1:T(8,128)}) %reduce-scatter.19.cloned.1.call-update) | async-done | bytes 32784 | tf_op jit(solution)/shard_map/reduce_scatter | solution.py:307
  1910.3 188.2 %reduce-scatter.17.cloned.1.call-done = f32[8,512,512]{2,1,0:T(8,128)} async-done(((f32[8,1024,512]{2,1,0:T(8,128)}), f32[8,512,512]{2,1,0:T(8,128)}) %reduce-scatter.17.cloned.1.call-update) | async-done | bytes 8388624 | tf_op jit(solution)/shard_map/reduce_scatter | solution.py:278
  2098.5 9.9 add_add_fusion.2
  (260 shorter events, 390.9 us)
Async XLA Ops:
  8.0 109.1 %all-gather.8.cloned.1.call-start = ((), (), s32[]{:S(2)}) async-start(), calls=%async_computation.8 | async-start | bytes 12582912 | tf_op jit(solution)/shard_map/all_gather | solution.py:255
  8.8 466.7 %reduce-scatter.11.cloned.1.call-start = ((), (), s32[]{:S(2)}) async-start(), calls=%async_computation.9 | async-start | bytes 25165824 | tf_op jit(solution)/shard_map/reduce_scatter | solution.py:258
  55.2 74.9 %copy-start.8 = (bf16[512,3,256]{2,0,1:T(8,128)(2,1)}, bf16[512,3,256]{2,0,1:T(8,128)(2,1)S(1)}, u32[]{:S(2)}) copy-start(bf16[512,3,256]{2,0,1:T(8,128)(2,1)S(1)} %all_gather.28) | copy-start | bytes 2359300
  141.5 134.3 %copy-start.6 = (bf16[256,512]{0,1:T(8,128)(2,1)S(1)}, bf16[256,512]{0,1:T(8,128)(2,1)}, u32[]{:S(2)}) copy-start(bf16[256,512]{0,1:T(8,128)(2,1)} %all_gather.29) | copy-start | bytes 786436
  286.1 2.0 copy-start.29
  286.2 201.8 %all-gather.12.cloned.1.call-start = ((), (), s32[]{:S(2)}) async-start(), calls=%async_computation.11 | async-start | bytes 1114112 | tf_op jit(solution)/shard_map/all_gather | solution.py:248
  287.7 303.4 %all-gather.10.cloned.1.call-start = ((), (), s32[]{:S(2)}) async-start(), calls=%async_computation.10 | async-start | bytes 12582912 | tf_op jit(solution)/shard_map/all_gather | solution.py:261
  480.9 3.4 copy-start
  484.3 2.8 copy-start.10
  487.1 207.6 %all-gather.14.cloned.1.call-start = ((), (), s32[]{:S(2)}) async-start(), calls=%async_computation.12 | async-start | bytes 1114112 | tf_op jit(solution)/shard_map/all_gather | solution.py:249
  487.8 412.4 %reduce-scatter.13.cloned.1.call-start = ((), (), s32[]{:S(2)}) async-start(), calls=%async_computation.13 | async-start | bytes 25165824 | tf_op jit(solution)/shard_map/reduce_scatter | solution.py:264
  711.0 322.2 %all-gather.16.cloned.1.call-start = ((), (), s32[]{:S(2)}) async-start(), calls=%async_computation.14 | async-start | bytes 12582912 | tf_op jit(solution)/shard_map/all_gather | solution.py:267
  913.4 11.1 copy-start.1
  913.4 6.8 copy-start.3
  920.2 4.3 copy-start.4
  924.5 108.7 %copy-start.34 = (bf16[1024,512]{0,1:T(8,128)(2,1)S(1)}, bf16[1024,512]{0,1:T(8,128)(2,1)}, u32[]{:S(2)}) copy-start(bf16[1024,512]{0,1:T(8,128)(2,1)} %all-gather.14.cloned.1.call-done) | copy-start | bytes 3145732
  929.0 341.2 %reduce-scatter.15.cloned.1.call-start = ((), (), s32[]{:S(2)}) async-start(), calls=%async_computation.15 | async-start | bytes 25165824 | tf_op jit(solution)/shard_map/reduce_scatter | solution.py:270
  1033.2 32.1 %copy-start.33 = (bf16[512,1024]{1,0:T(8,128)(2,1)S(1)}, bf16[512,1024]{1,0:T(8,128)(2,1)}, u32[]{:S(2)}) copy-start(bf16[512,1024]{1,0:T(8,128)(2,1)} %all-gather.12.cloned.1.call-done) | copy-start | bytes 3145732
  1081.0 189.2 %copy-start.28 = (f32[1,512]{1,0:T(1,128)S(1)}, f32[1,512]{1,0:T(1,128)}, u32[]{:S(2)}) copy-start(f32[1,512]{1,0:T(1,128)} %get-tuple-element.249) | copy-start | bytes 6148
  1081.1 320.9 %all-gather.18.cloned.1.call-start = ((), (), s32[]{:S(2)}) async-start(), calls=%async_computation.16 | async-start | bytes 12582912 | tf_op jit(solution)/shard_map/all_gather | solution.py:273
  1270.2 15.3 copy-start.16
  1285.5 9.4 copy-start.5
  1291.6 3.4 copy-start.2
  1291.6 3.4 copy-start.17
  1297.5 477.6 %reduce-scatter.23.cloned.1.call-start = ((), (), s32[]{:S(2)}) async-start(), calls=%async_computation.20 | async-start | bytes 2228224 | tf_op jit(solution)/shard_map/reduce_scatter | solution.py:309
  1314.0 16.7 copy-start.36
  1314.0 88.0 %copy-start.7 = (bf16[256,512]{0,1:T(8,128)(2,1)S(1)}, bf16[256,512]{0,1:T(8,128)(2,1)}, u32[]{:S(2)}) copy-start(bf16[256,512]{0,1:T(8,128)(2,1)} %all_gather.29) | copy-start | bytes 786436
  1314.0 462.8 %reduce-scatter.21.cloned.1.call-start = ((), (), s32[]{:S(2)}) async-start(), calls=%async_computation.19 | async-start | bytes 2228224 | tf_op jit(solution)/shard_map/reduce_scatter | solution.py:308
  1330.6 447.9 %reduce-scatter.25.cloned.1.call-start = ((), (), s32[]{:S(2)}) async-start(), calls=%async_computation.21 | async-start | bytes 278528
  1340.4 508.4 %all-reduce.4.cloned.1.call-start = ((), (), s32[]{:S(2)}) async-start(), calls=%async_computation.22 | async-start | bytes 4194304
  1751.0 9.0 copy-start.9
  1751.0 157.1 %reduce-scatter.19.cloned.1.call-start = ((), (), s32[]{:S(2)}) async-start(), calls=%async_computation.18 | async-start | bytes 557056 | tf_op jit(solution)/shard_map/reduce_scatter | solution.py:307
  1760.0 338.5 %reduce-scatter.17.cloned.1.call-start = ((), (), s32[]{:S(2)}) async-start(), calls=%async_computation.17 | async-start | bytes 25165824 | tf_op jit(solution)/shard_map/reduce_scatter | solution.py:278
  1773.2 1.9 copy-start.19
  1773.2 1.9 copy-start.20
  1773.2 3.6 copy-start.13
  1773.2 3.6 copy-start.21
  1773.2 3.6 copy-start.22
  1773.3 6.1 copy-start.30
  1773.3 6.1 copy-start.31
  1773.3 6.1 copy-start.32
  1773.3 134.8 %copy-start.23 = (f32[256,32]{0,1:T(8,128)S(1)}, f32[256,32]{0,1:T(8,128)}, u32[]{:S(2)}) copy-start(f32[256,32]{0,1:T(8,128)} %param.30) | copy-start | bytes 98308
  1773.3 134.8 %copy-start.26 = (f32[256,32]{0,1:T(8,128)S(1)}, f32[256,32]{0,1:T(8,128)}, u32[]{:S(2)}) copy-start(f32[256,32]{0,1:T(8,128)} %param.37) | copy-start | bytes 98308
  1773.3 134.8 %copy-start.27 = (f32[256,32]{0,1:T(8,128)S(1)}, f32[256,32]{0,1:T(8,128)}, u32[]{:S(2)}) copy-start(f32[256,32]{0,1:T(8,128)} %param.36) | copy-start | bytes 98308
  1773.3 136.2 %copy-start.14 = (f32[32,3,256]{2,0,1:T(8,128)S(1)}, f32[32,3,256]{2,0,1:T(8,128)}, u32[]{:S(2)}) copy-start(f32[32,3,256]{2,0,1:T(8,128)} %param.29) | copy-start | bytes 294916
  1773.3 136.2 %copy-start.24 = (f32[32,3,256]{2,0,1:T(8,128)S(1)}, f32[32,3,256]{2,0,1:T(8,128)}, u32[]{:S(2)}) copy-start(f32[32,3,256]{2,0,1:T(8,128)} %param.35) | copy-start | bytes 294916
  1773.4 136.2 %copy-start.25 = (f32[32,3,256]{2,0,1:T(8,128)S(1)}, f32[32,3,256]{2,0,1:T(8,128)}, u32[]{:S(2)}) copy-start(f32[32,3,256]{2,0,1:T(8,128)} %param.34) | copy-start | bytes 294916
  1773.4 325.1 %copy-start.18 = (f32[8,512]{1,0:T(8,128)S(1)}, f32[8,512]{1,0:T(8,128)}, u32[]{:S(2)}) copy-start(f32[8,512]{1,0:T(8,128)} %copy-done.17) | copy-start | bytes 49156
  (4 other events, 4.7 us)
Sparse Core Ops, SparseCore 0:
  10.4 106.6 all-gather.7
  286.3 189.1 reduce-scatter.10
  929.2 103.9 all-gather.15
  1297.6 104.3 all-gather.17
Sparse Core Ops, SparseCore 1:
  289.6 38.1 all-gather.11
  487.2 103.8 all-gather.9
  593.9 38.0 all-gather.13
  711.0 189.1 reduce-scatter.12
  1081.1 189.0 reduce-scatter.14
  1314.1 61.4 reduce-scatter.22
  1379.2 60.5 reduce-scatter.20
  1443.5 54.4 reduce-scatter.24
  1751.1 97.7 all-reduce.3
  1852.5 55.6 reduce-scatter.18
  1910.4 188.0 reduce-scatter.16
where the time goes:
time: 2130 us; the launch traced here: 2120 us
  waiting for transfers between devices  1190 us (56%)
  matrix products  498 us (23%)
  other arithmetic  265 us (12%)
  blocking collectives  73.7 us (3%)
  local copies, waits for them, and re-layouts  69.3 us (3%)
    reduce_scatter x1, waiting for transfers between devices, sum_feed(): return lax.psum_scatter(value, 'mp', scatter_dimension=1, tiled=True)  189 us
    reduce_scatter x1, waiting for transfers between devices, sum_normed(): return lax.psum_scatter(value, 'mp', scatter_dimension=1, tiled=True)  189 us
    reduce_scatter x1, waiting for transfers between devices, sum_input(): lax.psum_scatter(value, 'mp', scatter_dimension=1, tiled=True)  188 us
    reduce_scatter x1, waiting for transfers between devices, sum_attention(): return lax.psum_scatter(value, 'mp', scatter_dimension=1, tiled=True)  165 us
    all_gather x1, waiting for transfers between devices, gather_feed(): return lax.all_gather(value, 'mp', axis=1, tiled=True)  104 us
    all_gather x1, waiting for transfers between devices, gather_normed(): return lax.all_gather(value, 'mp', axis=1, tiled=True)  103 us
    dot_general x16, matrix products, masked_scores(): jnp.einsum('qhe,khe->hqk', query_rows, key_rows, preferred_element_type=j...  80.8 us
    convert_element_type x1, other arithmetic, layer_core(): active_backward = active_values.astype(jnp.bfloat16)  77.2 us
  transfers between devices with their start and end apart: 15, of which 10 were waited for; matrix products, arithmetic and copies ran while one was open for 25% of the time, Pallas kernels for 0%

commit v1 on v0

v1 whole, which is shorter than its diff:
```python
import functools

import jax
import jax.numpy as jnp
from jax import lax
from jax.experimental import pallas as pl
from jax.experimental.pallas import tpu as pltpu
from jax.sharding import PartitionSpec as P

STEP = 5
HD = 64
PAIR = 2 * HD
BLOCK = 256
CHUNK = 512
VMEM = 60 * 1024 * 1024

norm_eps = 1e-05
beta_first = 0.5
beta_second = 0.5
adam_eps = 1e-08
decay_rate = 0.01

FAR = 2.0**40
BITS = 7
EXTRA = 16
HEADS = 8

bf16 = jnp.bfloat16
f32 = jnp.float32


def dot_nn(a, b):
    return lax.dot_general(a, b, (((1,), (0,)), ((), ())), preferred_element_type=f32)


def dot_nt(a, b):
    return lax.dot_general(a, b, (((1,), (1,)), ((), ())), preferred_element_type=f32)


def dot_tn(a, b):
    return lax.dot_general(a, b, (((0,), (0,)), ((), ())), preferred_element_type=f32)


def params(**kw):
    return pltpu.CompilerParams(vmem_limit_bytes=VMEM, **kw)


def split_three(value):
    high = value.astype(bf16).astype(f32)
    rest = value - high
    middle = rest.astype(bf16).astype(f32)
    return high, middle, (rest - middle).astype(bf16).astype(f32)


def document_codes(segments):
    lane = jnp.arange(PAIR) % HD
    bit = (segments[..., None] >> (lane % BITS)) & 1
    low, high = lane < BITS, (lane >= BITS) & (lane < 2 * BITS)
    query = jnp.where(low, bit, jnp.where(high, 1 - bit, 0)).astype(bf16)
    key = jnp.where(low, 1 - bit, jnp.where(high, bit, 0)).astype(f32) * -FAR
    return query, key.astype(bf16)


def first_half(shape, axis):
    return lax.broadcasted_iota(jnp.int32, shape, axis) < HD


def head_lanes(head):
    lane = lax.broadcasted_iota(jnp.int32, (1, PAIR), 1) % HD
    mine = (lane == EXTRA + head) | (lane == EXTRA + HEADS + head) | (lane == EXTRA + 2 * HEADS + head)
    return mine.astype(f32).astype(bf16)


def attend_forward_kernel(x_ref, w_ref, qc_ref, kc_ref, q_ref, k_ref, v_ref, a_ref, mix_ref, lse_ref):
    length, width = x_ref.shape[1], x_ref.shape[2]
    x = x_ref[0]
    q = dot_nn(x, w_ref[:, 0:width]).astype(bf16)
    q_ref[0] = q * jnp.asarray(HD**-0.5, bf16)
    k_ref[0] = dot_nn(x, w_ref[:, width : 2 * width]).astype(bf16)
    v_ref[0] = dot_nn(x, w_ref[:, 2 * width : 3 * width]).astype(bf16)
    block = min(BLOCK, length)
    heads = width // HD

    @pl.loop(0, width // PAIR)
    def _(pair):
        lanes = pl.ds(pl.multiple_of(pair * PAIR, PAIR), PAIR)
        q_pair, k_pair, v_pair = q_ref[0, :, lanes], k_ref[0, :, lanes], v_ref[0, :, lanes]
        q_code, k_code = qc_ref[0], kc_ref[0]
        v_turned = v_pair.T
        one = jnp.ones_like(v_turned)
        lane_half = first_half((length, PAIR), 1)
        row_half = first_half((PAIR, length), 0)
        out_half = first_half((PAIR, block), 0)
        causal = lax.broadcasted_iota(jnp.int32, (block, block), 0) <= lax.broadcasted_iota(
            jnp.int32, (block, block), 1
        )
        parts = []
        for odd in (0, 1):
            if odd:
                qa, ka = jnp.where(lane_half, q_code, q_pair), jnp.where(lane_half, k_code, k_pair)
                va = jnp.where(row_half, one, v_turned)
            else:
                qa, ka = jnp.where(lane_half, q_pair, q_code), jnp.where(lane_half, k_pair, k_code)
                va = jnp.where(row_half, v_turned, one)
            outs, logs = [], []
            for start in range(0, length, block):
                stop = start + block
                scores = dot_nt(ka[:stop], qa[start:stop])
                last = jnp.where(causal, scores[start:], -FAR)
                scores = jnp.concatenate([scores[:start], last], axis=0) if start else last
                top = jnp.max(scores, axis=0, keepdims=True)
                weights = jnp.exp(scores - top).astype(bf16)
                out = dot_nn(va[:, :stop], weights)
                total = out[0:1] if odd else out[HD : HD + 1]
                outs.append(out * (1.0 / total))
                logs.append(top + jnp.log(total))
            lse_ref[pl.ds(2 * pair + odd, 1), :] = jnp.concatenate(logs, axis=1)
            parts.append(outs)
        for at, (even, odd) in enumerate(zip(*parts)):
            mixed = jnp.where(out_half, even, odd)
            mix_ref[0, at * block : (at + 1) * block, lanes] = mixed.T.astype(bf16)

    high, middle, low = split_three(-lse_ref[...])
    edge = jnp.zeros((EXTRA, length), f32)
    tail = jnp.zeros((HD - EXTRA - 3 * heads, length), f32)
    rows = jnp.concatenate([edge, high, middle, low, tail], axis=0)
    a_ref[0] = (jnp.concatenate([rows, rows], axis=0).T + qc_ref[0].astype(f32)).astype(bf16)


def attend_forward(x, w, q_code, k_code):
    count, length, width = x.shape
    whole = lambda s: (0, 0)
    row = lambda s: (s, 0, 0)
    wide, narrow = pl.BlockSpec((1, length, width), row), pl.BlockSpec((1, length, PAIR), row)
    shape = jax.ShapeDtypeStruct((count, length, width), bf16)
    return pl.pallas_call(
        attend_forward_kernel,
        grid=(count,),
        in_specs=[wide, pl.BlockSpec(w.shape, whole), narrow, narrow],
        out_specs=[wide, wide, wide, narrow, wide],
        out_shape=[shape, shape, shape, jax.ShapeDtypeStruct((count, length, PAIR), bf16), shape],
        scratch_shapes=[pltpu.VMEM((width // HD, length), f32)],
        compiler_params=params(),
        name="attend_forward",
    )(x, w, q_code, k_code)


def attend_backward_kernel(
    x_ref, w_ref, kc_ref, q_ref, k_ref, v_ref, a_ref, mix_ref, go_ref, dx_ref, dw_ref, grads, delta_ref, dq_ref
):
    length, width = x_ref.shape[1], x_ref.shape[2]
    block = min(BLOCK, length)

    @pl.when(pl.program_id(0) == 0)
    def _():
        dw_ref[...] = jnp.zeros_like(dw_ref)

    product = go_ref[0].astype(f32) * mix_ref[0].astype(f32)
    high = product.astype(bf16)
    low = (product - high.astype(f32)).astype(bf16)
    lane = lax.broadcasted_iota(jnp.int32, (width, PAIR), 1) % HD
    head = lax.broadcasted_iota(jnp.int32, (width, PAIR), 0) // HD
    third = lane - EXTRA - head
    picks = ((third == 0) | (third == HEADS) | (third == 2 * HEADS)).astype(f32).astype(bf16)
    delta = -(dot_nn(high, picks) + dot_nn(low, picks))
    high, middle, low = split_three(delta)
    lane = lax.broadcasted_iota(jnp.int32, (length, PAIR), 1) % HD
    delta_ref[...] = jnp.where(
        lane < EXTRA + HEADS, high, jnp.where(lane < EXTRA + 2 * HEADS, middle, low)
    ).astype(bf16)

    @pl.loop(0, width // PAIR)
    def _(pair):
        lanes = pl.ds(pl.multiple_of(pair * PAIR, PAIR), PAIR)
        q_pair, k_pair, v_pair, go_pair = (r[0, :, lanes] for r in (q_ref, k_ref, v_ref, go_ref))
        a, k_code, minus = a_ref[0], kc_ref[0], delta_ref[...]
        q_turned, go_turned = q_pair.T, go_pair.T
        lane_half = first_half((length, PAIR), 1)
        row_half = first_half((PAIR, block), 0)
        causal = lax.broadcasted_iota(jnp.int32, (block, block), 0) >= lax.broadcasted_iota(
            jnp.int32, (block, block), 1
        )
        dk, dv = [], []
        for odd in (0, 1):
            mine = head_lanes(2 * pair + odd)
            sides = ((q_pair, a), (k_pair, k_code + mine), (v_pair, jnp.broadcast_to(mine, v_pair.shape)), (go_pair, minus))
            qa, ka, va, ga = (
                jnp.where(lane_half, other, own) if odd else jnp.where(lane_half, own, other) for own, other in sides
            )
            for at, start in enumerate(range(0, length, block)):
                stop = start + block
                scores = dot_nt(qa[start:], ka[start:stop])
                first = jnp.where(causal, scores[:block], -FAR)
                scores = jnp.concatenate([first, scores[block:]], axis=0) if stop < length else first
                probs = jnp.exp(scores)
                dscores = (probs * dot_nt(ga[start:], va[start:stop])).astype(bf16)
                dv_at = dot_nn(go_turned[:, start:], probs.astype(bf16))
                dk_at = dot_nn(q_turned[:, start:], dscores)
                dq_at = dot_nn(dscores, k_pair[start:stop])
                if at:
                    dq_ref[odd, start:, :] += dq_at
                else:
                    dq_ref[odd] = dq_at
                if odd:
                    dv[at] = jnp.where(row_half, dv[at], dv_at)
                    dk[at] = jnp.where(row_half, dk[at], dk_at)
                else:
                    dv.append(dv_at)
                    dk.append(dk_at)
        dq = jnp.where(lane_half, dq_ref[0], dq_ref[1]) * HD**-0.5
        grads[:, lanes] = dq.astype(bf16)
        k_lanes = pl.ds(pl.multiple_of(width + pair * PAIR, PAIR), PAIR)
        v_lanes = pl.ds(pl.multiple_of(2 * width + pair * PAIR, PAIR), PAIR)
        for at, start in enumerate(range(0, length, block)):
            grads[start : start + block, k_lanes] = dk[at].T.astype(bf16)
            grads[start : start + block, v_lanes] = dv[at].T.astype(bf16)

    dx_ref[0] = dot_nt(grads[...], w_ref[...]).astype(bf16)
    dw_ref[...] += dot_tn(x_ref[0], grads[...])


def attend_backward(x, w, k_code, q, k, v, a, mix, go):
    count, length, width = x.shape
    whole = lambda s: (0, 0)
    row = lambda s: (s, 0, 0)
    wide, narrow = pl.BlockSpec((1, length, width), row), pl.BlockSpec((1, length, PAIR), row)
    return pl.pallas_call(
        attend_backward_kernel,
        grid=(count,),
        in_specs=[wide, pl.BlockSpec(w.shape, whole), narrow, wide, wide, wide, narrow, wide, wide],
        out_specs=[wide, pl.BlockSpec(w.shape, whole)],
        out_shape=[jax.ShapeDtypeStruct((count, length, width), bf16), jax.ShapeDtypeStruct(w.shape, f32)],
        scratch_shapes=[
            pltpu.VMEM((length, 3 * width), bf16),
            pltpu.VMEM((length, PAIR), bf16),
            pltpu.VMEM((2, length, PAIR), f32),
        ],
        compiler_params=params(),
        name="attend_backward",
    )(x, w, k_code, q, k, v, a, mix, go)


def normalize(rows):
    center = rows - jnp.mean(rows, axis=-1, keepdims=True)
    rstd = lax.rsqrt(jnp.mean(center * center, axis=-1, keepdims=True) + norm_eps)
    return center * rstd, rstd


def normalize_back(grad, xhat, rstd, gain):
    scaled = grad * gain
    return rstd * (
        scaled - jnp.mean(scaled, axis=-1, keepdims=True) - xhat * jnp.mean(scaled * xhat, axis=-1, keepdims=True)
    )


def token_kernel(n_prev, *refs):
    ids_ref, x_ref, d_ref, cx_ref, cd_ref, mix_ref, out_ref, in_ref, back_ref, norm_ref = refs[:10]
    xo_ref, do_ref, gr_ref, act_ref, gh_ref, xb_ref, gf_ref, gb_ref, mo_ref, gm_ref, ng_ref, slope = refs[10 + n_prev :]
    hidden = in_ref.shape[1]
    chunk = min(CHUNK, hidden)

    @pl.when(pl.program_id(0) == 0)
    def _():
        ng_ref[...] = jnp.zeros_like(ng_ref)

    g1, b1, g2, b2 = (norm_ref[i : i + 1] for i in range(4))
    mix = mix_ref[0]
    mo_ref[0] = mix
    attended = dot_nt(mix, out_ref[...])
    xhat1, rstd1 = normalize(x_ref[0].astype(f32) + attended)
    x_one = xhat1 * g1 + b1
    xb = x_one.astype(bf16)
    xb_ref[0] = xb
    feed = None
    for at in range(0, hidden, chunk):
        cols = slice(at, at + chunk)
        h = dot_nn(xb, in_ref[:, cols])
        cdf = 0.5 * lax.erf(h * 0.7071067811865476) + 0.5
        active = (h * cdf).astype(bf16)
        act_ref[0, :, cols] = active
        slope[:, cols] = cdf + h * (jnp.exp(-0.5 * (h * h)) * 0.3989422804014327)
        part = dot_nt(active, back_ref[:, cols])
        feed = part if feed is None else feed + part
    xhat2, rstd2 = normalize(x_one + feed)
    xo_ref[0] = (xhat2 * g2 + b2).astype(bf16)
    do_ref[0] = (d_ref[0].astype(f32) + attended + feed).astype(bf16)
    cx, cd = cx_ref[0].astype(f32), cd_ref[0].astype(f32)
    grad_r2 = normalize_back(cx, xhat2, rstd2, g2)
    dg2, db2 = jnp.sum(cx * xhat2, axis=0, keepdims=True), jnp.sum(cx, axis=0, keepdims=True)
    gf = (grad_r2 + cd).astype(bf16)
    gf_ref[0] = gf
    grad_x1 = grad_r2
    for at in range(0, hidden, chunk):
        cols = slice(at, at + chunk)
        gh = (dot_nn(gf, back_ref[:, cols]) * slope[:, cols]).astype(bf16)
        gh_ref[0, :, cols] = gh
        grad_x1 = grad_x1 + dot_nt(gh, in_ref[:, cols])
    grad_r1 = normalize_back(grad_x1, xhat1, rstd1, g1)
    gr_ref[0] = grad_r1
    dg1, db1 = jnp.sum(grad_x1 * xhat1, axis=0, keepdims=True), jnp.sum(grad_x1, axis=0, keepdims=True)
    ng_ref[...] += jnp.concatenate([dg1, db1, dg2, db2, jnp.zeros((4, dg1.shape[1]), f32)], axis=0)
    gb = (grad_r1 + cd).astype(bf16)
    gb_ref[0] = gb
    gm_ref[0] = dot_nn(gb, out_ref[...]).astype(bf16)


def token_block(ids, first, mix, x, d, cot_x, cot_d, out_turned, w_in, back_turned, norms, prev):
    count, rows, width = mix.shape
    total, hidden = x.shape[0], w_in.shape[1]
    there = lambda s, ids: (ids[s], 0, 0)
    here = lambda s, ids: (s, 0, 0)
    after = lambda s, ids: (s + first, 0, 0)
    whole = lambda s, ids: (0, 0)
    one = (1, rows, width)
    full = lambda n, dtype: jax.ShapeDtypeStruct((total, rows, n), dtype)
    shapes = [
        full(width, bf16),
        full(width, bf16),
        full(width, f32),
        full(hidden, bf16),
        full(hidden, bf16),
        full(width, bf16),
        full(width, bf16),
        full(width, bf16),
        full(width, bf16),
    ]
    specs = [pl.BlockSpec(one, there)] * 3
    specs += [pl.BlockSpec((1, rows, hidden), after)] * 2 + [pl.BlockSpec(one, after)] * 4
    weights = [pl.BlockSpec(w.shape, whole) for w in (out_turned, w_in, back_turned, norms)]
    out = pl.pallas_call(
        functools.partial(token_kernel, len(prev)),
        grid_spec=pltpu.PrefetchScalarGridSpec(
            num_scalar_prefetch=1,
            grid=(count,),
            in_specs=[pl.BlockSpec(one, there)] * 4
            + [pl.BlockSpec(one, here)]
            + weights
            + [pl.BlockSpec(memory_space=pl.ANY)] * len(prev),
            out_specs=specs + [pl.BlockSpec(one, here), pl.BlockSpec((8, width), whole)],
            scratch_shapes=[pltpu.VMEM((rows, hidden), f32)],
        ),
        out_shape=shapes
        + [jax.ShapeDtypeStruct((count, rows, width), bf16), jax.ShapeDtypeStruct((8, width), f32)],
        input_output_aliases={10 + i: i for i in range(len(prev))},
        compiler_params=params(),
        name="token_block",
    )(ids, x, d, cot_x, cot_d, mix, out_turned, w_in, back_turned, norms, *prev)
    return out[:9], out[9], out[10]


def weight_kernel(act_ref, gh_ref, xb_ref, gf_ref, gb_ref, mo_ref, out_ref, in_ref, back_ref):
    @pl.when(pl.program_id(0) == 0)
    def _():
        out_ref[...] = jnp.zeros_like(out_ref)
        in_ref[...] = jnp.zeros_like(in_ref)
        back_ref[...] = jnp.zeros_like(back_ref)

    back_ref[...] += dot_tn(gf_ref[0], act_ref[0])
    in_ref[...] += dot_tn(xb_ref[0], gh_ref[0])
    out_ref[...] += dot_tn(gb_ref[0], mo_ref[0])


def weight_gradients(act, gh, xb, gf, gb, mo):
    total, rows, hidden = act.shape
    width = xb.shape[2]
    row = lambda s: (s, 0, 0)
    whole = lambda s: (0, 0)
    wide, narrow = pl.BlockSpec((1, rows, hidden), row), pl.BlockSpec((1, rows, width), row)
    shapes = [(width, width), (width, hidden), (width, hidden)]
    return pl.pallas_call(
        weight_kernel,
        grid=(total,),
        in_specs=[wide, wide, narrow, narrow, narrow, narrow],
        out_specs=[pl.BlockSpec(s, whole) for s in shapes],
        out_shape=[jax.ShapeDtypeStruct(s, f32) for s in shapes],
        compiler_params=params(),
        name="weight_gradients",
    )(act, gh, xb, gf, gb, mo)


def adam_update(weight, grad, mom, sec, rate):
    mom_new = beta_first * mom + (1.0 - beta_first) * grad
    sec_new = beta_second * sec + (1.0 - beta_second) * grad * grad
    scaled = (
        mom_new
        / (1.0 - beta_first**STEP)
        / (jnp.sqrt(sec_new / (1.0 - beta_second**STEP)) + adam_eps)
    )
    return (mom_new, sec_new, weight - rate * (scaled + decay_rate * weight))


def swap(value):
    return lax.ppermute(value, "mp", [(0, 1), (1, 0)])


def on_device(
    x_in,
    d_in,
    segments,
    cot_x,
    cot_d,
    w_qkv,
    w_out,
    w_in,
    w_back,
    norms,
    qkv_mom,
    qkv_sec,
    out_mom,
    out_sec,
    in_mom,
    in_sec,
    back_mom,
    back_sec,
    norm_mom,
    norm_sec,
):
    parts, owners = lax.axis_size("mp"), lax.axis_size("dp")
    me = lax.axis_index("mp")
    total, rows, width = x_in.shape
    mine = total // parts
    length = rows * parts
    own_rows = w_qkv.shape[0]
    here = lambda v, start, count: lax.dynamic_slice_in_dim(v, start, count, axis=0)

    def gather(shard):
        got = lax.all_gather(shard.astype(bf16), ("dp", "mp"), axis=0)
        return got.reshape((owners, parts) + shard.shape)

    qkv = gather(w_qkv).transpose(0, 2, 3, 1, 4).reshape(width, 3 * width)
    n_out, n_in, n_back = w_out.shape[0], w_in.shape[1], w_back.shape[0]
    rest = gather(jnp.concatenate([w_out.T, w_in, w_back.T], axis=1)).transpose(0, 2, 1, 3)
    rest = rest.reshape(width, parts, n_out + n_in + n_back)
    out_turned = rest[:, :, :n_out].reshape(width, parts * n_out)
    in_whole = rest[:, :, n_out : n_out + n_in].reshape(width, parts * n_in)
    back_turned = rest[:, :, n_out + n_in :].reshape(width, parts * n_back)
    gain_rows = lax.all_gather(norms.astype(bf16), "dp", axis=1, tiled=True).astype(f32)

    q_code, k_code = document_codes(here(segments, me * mine, mine))

    def tokens(ids, first, mix, prev):
        return token_block(
            ids, first, mix, x_in, d_in, cot_x, cot_d, out_turned, in_whole, back_turned, gain_rows, prev
        )

    if parts == 2:
        other = 1 - me
        step = max(mine // 2, 1)
        chunks = list(range(0, mine, step))

        def join(own, got):
            return jnp.where(me == 0, jnp.concatenate([own, got], axis=1), jnp.concatenate([got, own], axis=1))

        forward = []
        for at in chunks:
            got = swap(here(x_in, other * mine + at, step))
            x_whole = join(here(x_in, me * mine + at, step), got)
            q, k, v, a, mix = attend_forward(x_whole, qkv, q_code[at : at + step], k_code[at : at + step])
            halves = mix.reshape(step, parts, rows, width)
            pick = lambda i, halves=halves: lax.dynamic_index_in_dim(halves, i, axis=1, keepdims=False)
            forward.append((x_whole, q, k, v, a, mix, pick(me), swap(pick(other))))
        spread = jnp.arange(mine, dtype=jnp.int32)
        own_mix = jnp.concatenate([f[6] for f in forward], axis=0)
        prev, own_gm, norm_grad = tokens(me * mine + spread, 0, own_mix, ())
        got_gm = []
        for i, at in enumerate(chunks):
            prev, gm, ng = tokens(other * mine + at + spread[:step], mine + at, forward[i][7], prev)
            norm_grad = norm_grad + ng
            got_gm.append(swap(gm))
        x_out, d_out, grad_r1, act, gh, xb, gf, gb, mo = prev
        token_grads = weight_gradients(act, gh, xb, gf, gb, mo)
        qkv_grad, own_dx, got_dx = 0.0, [], []
        for i, at in enumerate(chunks):
            x_whole, q, k, v, a, mix = forward[i][:6]
            go = join(own_gm[at : at + step], got_gm[i])
            dx, dw = attend_backward(x_whole, qkv, k_code[at : at + step], q, k, v, a, mix, go)
            halves = dx.reshape(step, parts, rows, width)
            pick = lambda i, halves=halves: lax.dynamic_index_in_dim(halves, i, axis=1, keepdims=False)
            own_dx.append(pick(me))
            got_dx.append(swap(pick(other)))
            qkv_grad = qkv_grad + dw
        own_dx, got_dx = jnp.concatenate(own_dx, axis=0), jnp.concatenate(got_dx, axis=0)
        dx = jnp.where(
            me == 0, jnp.concatenate([own_dx, got_dx], axis=0), jnp.concatenate([got_dx, own_dx], axis=0)
        )
    else:

        def to_sequences(v):
            got = lax.all_to_all(v.reshape(parts, mine, rows, width), "mp", 0, 0)
            return got.transpose(1, 0, 2, 3).reshape(mine, length, width)

        def to_positions(v):
            sent = v.reshape(mine, parts, rows, width).transpose(1, 0, 2, 3)
            return lax.all_to_all(sent, "mp", 0, 0).reshape(total, rows, width)

        x_whole = to_sequences(x_in)
        q, k, v, a, mix = attend_forward(x_whole, qkv, q_code, k_code)
        prev, gm, norm_grad = tokens(jnp.arange(total, dtype=jnp.int32), 0, to_positions(mix), ())
        x_out, d_out, grad_r1, act, gh, xb, gf, gb, mo = prev
        token_grads = weight_gradients(act, gh, xb, gf, gb, mo)
        dx, qkv_grad = attend_backward(x_whole, qkv, k_code, q, k, v, a, mix, to_sequences(gm))
        dx = to_positions(dx)
    x_grad = grad_r1 + dx.astype(f32)

    def scatter(value):
        n = value.shape[1] // parts
        blocks = value.astype(bf16).reshape(width, parts, n)
        got = lax.psum_scatter(blocks, "dp", scatter_dimension=0, tiled=True)
        return lax.psum_scatter(got, "mp", scatter_dimension=1, tiled=True)[:, 0].astype(f32)

    out_g, in_g, back_g = token_grads
    n_all = n_out + n_in + n_back
    packed = jnp.concatenate(
        [
            out_g.reshape(width, parts, n_out),
            in_g.reshape(width, parts, n_in),
            back_g.reshape(width, parts, n_back),
        ],
        axis=2,
    ).reshape(width, parts * n_all)
    got = scatter(packed)
    out_g, in_g, back_g = got[:, :n_out].T, got[:, n_out : n_out + n_in], got[:, n_out + n_in :].T
    qkv_n = w_qkv.shape[2]
    qkv_packed = qkv_grad.reshape(width, 3, parts, qkv_n).transpose(0, 2, 1, 3).reshape(width, parts * 3 * qkv_n)
    qkv_g = scatter(qkv_packed).reshape(own_rows, 3, qkv_n)
    norm_g = lax.psum_scatter(
        lax.psum(norm_grad[:4], "mp"), "dp", scatter_dimension=1, tiled=True
    )
    qkv_state = adam_update(w_qkv, qkv_g, qkv_mom, qkv_sec, 0.05)
    out_state = adam_update(w_out, out_g, out_mom, out_sec, 0.3)
    in_state = adam_update(w_in, in_g, in_mom, in_sec, 0.05)
    back_state = adam_update(w_back, back_g, back_mom, back_sec, 0.025)
    norm_state = adam_update(norms, norm_g, norm_mom, norm_sec, 0.1)
    return (x_out, d_out, x_grad, *qkv_state, *out_state, *in_state, *back_state, *norm_state)


def solution(mesh):
    stream = P("dp", "mp", None)
    weights = (P("dp", None, "mp"), P("mp", "dp"), P("dp", "mp"), P("mp", "dp"), P(None, "dp"))
    states = tuple(spec for spec in weights for _ in range(2))
    news = tuple(spec for spec in weights for _ in range(3))
    return jax.shard_map(
        on_device,
        mesh=mesh,
        in_specs=(stream, stream, P("dp", None), stream, stream) + weights + states,
        out_specs=(stream, stream, stream) + news,
        check_vma=False,
    )
```

time: 2130 us -> 636 us (0.30)
  waiting for transfers between devices: 1190 us -> 215 us
  matrix products: 498 us -> 0 us
  Pallas kernels: 0 us -> 260 us
  other arithmetic: 265 us -> 47.1 us
  blocking collectives: 73.7 us -> 27 us
    reduce_scatter x7 -> x3, waiting for transfers between devices: 790 us -> 88.7 us  [the longest x1 76.8 us: scatter(): got = lax.psum_scatter(blocks, 'dp', scatter_dimension=0, tiled=True)]
    dot_general x68 -> x0, matrix products: 498 us -> none  [the longest x16 80.8 us: masked_scores(): jnp.einsum('qhe,khe->hqk', query_rows, key_rows, preferred_element_type=j...]
    all_gather x6 -> x2, waiting for transfers between devices: 331 us -> 0.01 us  [gather(): got = lax.all_gather(shard.astype(bf16), ('dp', 'mp'), axis=0)]
    pallas_call x0 -> x8, Pallas kernels: none -> 260 us  [the longest x2 86.3 us: attend_backward(): pl.pallas_call(attend_backward_kernel, grid=(count,), in_specs=[wide, pl....]
    convert_element_type x17 -> x6, other arithmetic: 152 us -> 7.36 us  [the longest x1 3.28 us: scatter(): blocks = value.astype(bf16).reshape(width, parts, n)]
    reduce_sum x15 -> x0, other arithmetic: 81.6 us -> none  [the longest x8 29.3 us: attend_forward(): total = jnp.sum(exponent, axis=-1, keepdims=True)]
    all_gather x3 -> x1, blocking collectives: 66.1 us -> 22.1 us  [on_device(): lax.all_gather(norms.astype(bf16), 'dp', axis=1, tiled=True).astype(f32)]
    unnamed x17 -> x9, waiting for transfers between devices: 69.8 us -> 105 us
  transfers between devices with their start and end apart: 15 -> 15, of which waited for: 10 -> 7; matrix products, arithmetic and copies ran while one was open for 25% -> 12% of each run, Pallas kernels for 0% -> 34%
where the time goes in v1:
time: 636 us; the launch traced here: 628 us
  Pallas kernels  260 us (41%)
  waiting for transfers between devices  215 us (34%)
  local copies, waits for them, and re-layouts  53.6 us (8%)
  other arithmetic  47.1 us (7%)
  blocking collectives  27 us (4%)
  between operations  15.6 us (2%)
  starting transfers between devices  9.87 us (2%)
    unnamed x9, waiting for transfers between devices  105 us
    pallas_call x2, Pallas kernels, attend_backward(): pl.pallas_call(attend_backward_kernel, grid=(count,), in_specs=[wide, pl....  86.3 us
    reduce_scatter x1, waiting for transfers between devices, scatter(): got = lax.psum_scatter(blocks, 'dp', scatter_dimension=0, tiled=True)  76.8 us
    pallas_call x3, Pallas kernels, token_block(): pl.pallas_call(functools.partial(token_kernel, len(prev)), grid_spec=pltp...  76.4 us
    pallas_call x2, Pallas kernels, attend_forward(): pl.pallas_call(attend_forward_kernel, grid=(count,), in_specs=[wide, pl.B...  68.2 us
    pallas_call x1, Pallas kernels, weight_gradients(): pl.pallas_call(weight_kernel, grid=(total,), in_specs=[wide, wide, narrow...  28.6 us
    all_gather x1, blocking collectives, on_device(): lax.all_gather(norms.astype(bf16), 'dp', axis=1, tiled=True).astype(f32)  22.1 us
    ppermute x8, waiting for transfers between devices, swap(): return lax.ppermute(value, 'mp', [(0, 1), (1, 0)])  21 us
  transfers between devices with their start and end apart: 15, of which 7 were waited for; matrix products, arithmetic and copies ran while one was open for 12% of the time, Pallas kernels for 34%

profile of v1, /device:TPU:0, one launch (start us, length us, event | category | flops | bytes accessed | tf_op | source)
XLA Modules:
  0.0 627.8 jit_solution(2323930537121630822)
XLA Ops:
  7.3 1.5 convert_element_type.57
  12.2 3.9 constant_dynamic-slice_fusion.1
  16.1 3.0 collective-permute-start.2
  19.1 22.1 %all-gather.1 = bf16[16,32,4]{1,2,0:T(4,128)(2,1)S(1)} all-gather(bf16[1,32,4]{1,2,0:T(4,128)(2,1)S(1)} %convert_bitcast_fusion.3), channel_id=1, replica_groups=mesh['dp'=16,'mp'=2] {'dp'}, dimensions={0}, use_global_device_ids=true | all-gather | bytes 4352 | tf_op jit(solution)/shard_map/all_gather | solution.py:437
  46.7 3.4 maximum_select_fusion.2.x_ref
  50.2 18.6 %collective-permute-done = bf16[2,512,512]{2,1,0:T(8,128)(2,1)} collective-permute-done((bf16[2,512,512]{2,1,0:T(8,128)(2,1)}, bf16[2,512,512]{2,1,0:T(8,128)(2,1)}, u32[]{:S(2)}, u32[]{:S(2)}) %collective-permute-start) | collective-permute-done | bytes 1048608 | tf_op jit(solution)/shard_map/ppermute | solution.py:393
  68.8 3.6 maximum_select_fusion.1.x_ref
  72.4 3.0 copy.180
  75.4 2.0 reshape.157.w_ref
  77.3 34.1 %attend_forward.3 = (bf16[2,1024,512]{2,1,0:T(8,128)(2,1)}, bf16[2,1024,512]{2,1,0:T(8,128)(2,1)}, bf16[2,1024,512]{2,1,0:T(8,128)(2,1)}, bf16[2,1024,128]{2,1,0:T(8,128)(2,1)}, bf16[2,1024,512]{2,1,0:T(8,128)(2,1)}) custom-call(bf16[2,1024,512]{2,1,0:T(8,128)(2,1)} %maximum_select_fusion.2.x_ref, bf16[512,1536]{1,0:T(8,128)(2,1)} %reshape.157.w_ref, ...), custom_call_target="tpu_custom_call" | custom-call | tf_op jit(solution)/shard_map/attend_forward/pallas_call | solution.py:136
  111.4 1.7 dynamic-slice_bitcast_fusion.5
  113.1 1.8 collective-permute-start.3
  114.9 34.2 %attend_forward.2 = (bf16[2,1024,512]{2,1,0:T(8,128)(2,1)}, bf16[2,1024,512]{2,1,0:T(8,128)(2,1)}, bf16[2,1024,512]{2,1,0:T(8,128)(2,1)}, bf16[2,1024,128]{2,1,0:T(8,128)(2,1)}, bf16[2,1024,512]{2,1,0:T(8,128)(2,1)}) custom-call(bf16[2,1024,512]{2,1,0:T(8,128)(2,1)} %maximum_select_fusion.1.x_ref, bf16[512,1536]{1,0:T(8,128)(2,1)} %reshape.157.w_ref, ...), custom_call_target="tpu_custom_call" | custom-call | tf_op jit(solution)/shard_map/attend_forward/pallas_call | solution.py:136
  149.1 1.7 dynamic-slice_bitcast_fusion.4
  151.1 1.5 pad_maximum_fusion.1.refs_5_
  152.6 9.4 %copy.144 = bf16[16,32,2,2304]{3,2,1,0:T(2,128)(2,1)} copy(bf16[16,32,2,2304]{3,1,2,0:T(8,128)(2,1)} %bitcast.119) | data formatting | bytes 9437184 | tf_op jit(solution)/shard_map/transpose | solution.py:432
  163.4 4.7 fusion.11
  168.1 1.9 copy.167
  170.0 2.1 copy.168
  173.0 34.7 %token_block.3 = (bf16[8,512,512]{2,1,0:T(8,128)(2,1)}, bf16[8,512,512]{2,1,0:T(8,128)(2,1)}, f32[8,512,512]{2,1,0:T(8,128)}, bf16[8,512,2048]{2,1,0:T(8,128)(2,...) custom-call(s32[4]{0:T(128)} %iota_add_fusion.refs_0_, ...), custom_call_target="tpu_custom_call" | custom-call | tf_op jit(solution)/shard_map/token_block/pallas_call | solution.py:330
  207.7 20.9 %token_block.4 = (bf16[8,512,512]{2,1,0:T(8,128)(2,1)}, bf16[8,512,512]{2,1,0:T(8,128)(2,1)}, f32[8,512,512]{2,1,0:T(8,128)}, bf16[8,512,2048]{2,1,0:T(8,128)(2,...) custom-call(s32[2]{0:T(128)} %get-tuple-element.225.refs_0_, ...), custom_call_target="tpu_custom_call", output_to_operand_aliasing={{0}: (10, {}), {1}: (11, {}), {2}: (12, {}), {3}: (13, {}),... | custom-call | tf_op jit(solution)/shard_map/token_block/pallas_call | solution.py:330
  228.7 1.8 collective-permute-start.4
  230.5 20.7 %token_block.5 = (bf16[8,512,512]{2,1,0:T(8,128)(2,1)}, bf16[8,512,512]{2,1,0:T(8,128)(2,1)}, f32[8,512,512]{2,1,0:T(8,128)}, bf16[8,512,2048]{2,1,0:T(8,128)(2,...) custom-call(s32[2]{0:T(128)} %get-tuple-element.226.refs_0_, ...), custom_call_target="tpu_custom_call", output_to_operand_aliasing={{0}: (10, {}), {1}: (11, {}), {2}: (12, {}), {3}: (13, {}),... | custom-call | tf_op jit(solution)/shard_map/token_block/pallas_call | solution.py:330
  251.7 2.4 collective-permute-done.4
  254.1 3.7 maximum_select_fusion.3.go_ref
  257.8 43.1 %attend_backward.2 = (bf16[2,1024,512]{2,1,0:T(8,128)(2,1)}, f32[512,1536]{1,0:T(8,128)}) custom-call(bf16[2,1024,512]{2,1,0:T(8,128)(2,1)} %maximum_select_fusion.2.x_ref, bf16[512,1536]{1,0:T(8,128)(2,1)} %reshape.157.w_ref, bf16[2,1024,128]{2,1,0:T(8,128)(2,1)} %get-tuple-element.221.kc_ref, bf16[2,1024,512]{2,1,0:T(8,128)(2,1)} %get-tuple-element.91.q_ref, ...), custom_call_target="tpu_custom_call" | custom-call | tf_op jit(solution)/shard_map/attend_backward/pallas_call | solution.py:227
  300.9 3.5 maximum_select_fusion.4.go_ref
  304.5 43.2 %attend_backward.3 = (bf16[2,1024,512]{2,1,0:T(8,128)(2,1)}, f32[512,1536]{1,0:T(8,128)}) custom-call(bf16[2,1024,512]{2,1,0:T(8,128)(2,1)} %maximum_select_fusion.1.x_ref, bf16[512,1536]{1,0:T(8,128)(2,1)} %reshape.157.w_ref, bf16[2,1024,128]{2,1,0:T(8,128)(2,1)} %get-tuple-element.222.kc_ref, bf16[2,1024,512]{2,1,0:T(8,128)(2,1)} %get-tuple-element.98.q_ref, ...), custom_call_target="tpu_custom_call" | custom-call | tf_op jit(solution)/shard_map/attend_backward/pallas_call | solution.py:227
  347.6 3.3 add_convert_fusion
  351.3 2.2 copy.149
  353.5 3.0 copy.150
  358.7 28.6 %weight_gradients.1 = (f32[512,512]{1,0:T(8,128)}, f32[512,2048]{1,0:T(8,128)}, f32[512,2048]{1,0:T(8,128)}) custom-call(bf16[8,512,2048]{2,1,0:T(8,128)(2,1)} %get-tuple-element.106.act_ref, bf16[8,512,2048]{2,1,0:T(8,128)(2,1)} %get-tuple-element.107.gh_ref, bf16[8,512,512]{2,1,0:T(8,128)(2,1)} %get-tuple-element.108.xb_ref, ...), custom_call_target="tpu_custom_call" | custom-call | tf_op jit(solution)/shard_map/weight_gradients/pallas_call | solution.py:370
  387.4 2.5 convert.33
  390.1 2.0 copy-done.2
  392.4 1.6 copy.179
  394.2 59.1 %all-reduce.3.cloned.1.call-done = bf16[512,2,768]{2,1,0:T(2,128)(2,1)} async-done(((bf16[512,2,768]{2,1,0:T(2,128)(2,1)}), bf16[512,2,768]{2,1,0:T(2,128)(2,1)}) %all-reduce.3.cloned.1.call-update) | async-done | bytes 1572880
  455.0 3.6 pad_maximum_fusion
  458.6 1.5 copy-done.3
  461.3 1.5 collective-permute-start.6
  464.8 46.1 %reduce-scatter.13.cloned.1.call-done = f32[32,4]{1,0:T(8,128)} async-done(((f32[512,4]{1,0:T(8,128)}), f32[32,4]{1,0:T(8,128)}) %reduce-scatter.13.cloned.1.call-update) | async-done | bytes 528
  511.7 4.9 psum.8
  517.2 5.3 reduce-scatter.7.cloned.1.call-done
  523.4 1.6 multiply_subtract_fusion.2
  525.1 76.8 %reduce-scatter.9.cloned.1.call-done = bf16[32,2,2304]{2,0,1:T(8,128)(2,1)} async-done(((bf16[512,2,2304]{2,0,1:T(8,128)(2,1)}), bf16[32,2,2304]{2,0,1:T(8,128)(2,1)}) %reduce-scatter.9.cloned.1.call-update) | async-done | bytes 294928 | tf_op jit(solution)/shard_map/reduce_scatter | solution.py:508
  601.9 6.8 %convert_add_fusion = f32[8,512,512]{2,1,0:T(8,128)} fusion(f32[8,512,512]{2,1,0:T(8,128)} %get-tuple-element.90, bf16[2,512,512]{2,1,0:T(8,128)(2,1)} %collective-permute-done.7, bf16[2,512,512]{2,1,0:T(8,128)(2,1)S(1)} %collective-permute-done.6, bf16[2,512,512]{2,1,0:T(8,128)(2,1)S(1)} %get-tuple-element.213, ...), kind=kLoop, calls=%fused_computation | loop fusion | flops 18874368 | bytes 20971520 | tf_op jit(solution)/shard_map/add | solution.py:503
  608.7 6.6 %reduce-scatter.11.cloned.1.call-done = bf16[32,1,2304]{2,0,1:T(8,128)(2,1)} async-done(((bf16[32,2,2304]{2,0,1:T(8,128)(2,1)}), bf16[32,1,2304]{2,0,1:T(8,128)(2,1)}) %reduce-scatter.11.cloned.1.call-update) | async-done | bytes 147472 | tf_op jit(solution)/shard_map/reduce_scatter | solution.py:509
  616.3 1.8 multiply_subtract_fusion
  618.0 1.8 multiply_subtract_fusion.1
  (103 shorter events, 23.5 us)
Async XLA Ops:
  7.2 34.0 %copy-start = (s32[8,1024]{1,0:T(8,128)S(1)}, s32[8,1024]{1,0:T(8,128)}, u32[]{:S(2)}) copy-start(s32[8,1024]{1,0:T(8,128)} %param.22) | copy-start | bytes 98308
  7.2 65.1 %all-gather.7.cloned.1.call-start = ((), (), s32[]{:S(2)}) async-start(), calls=%async_computation.8 | async-start | bytes 1622016 | tf_op jit(solution)/shard_map/all_gather | solution.py:427
  8.8 143.8 %all-gather.5.cloned.1.call-start = ((), (), s32[]{:S(2)}) async-start(), calls=%async_computation.4 | async-start | bytes 4866048 | tf_op jit(solution)/shard_map/all_gather | solution.py:427
  12.1 441.1 %all-reduce.3.cloned.1.call-start = ((), (), s32[]{:S(2)}) async-start(), calls=%async_computation.10 | async-start | bytes 3145728
  12.2 6.9 %copy-start.14 = (f32[4,32]{1,0:T(4,128)S(1)}, f32[4,32]{1,0:T(4,128)}, u32[]{:S(2)}) copy-start(f32[4,32]{1,0:T(4,128)} %param.29) | copy-start | bytes 1540
  16.1 30.6 %collective-permute-start.2 = (bf16[2,512,512]{2,1,0:T(8,128)(2,1)}, bf16[2,512,512]{2,1,0:T(8,128)(2,1)}, u32[]{:S(2)}, u32[]{:S(2)}) collective-permute-start(bf16[2,512,512]{2,1,0:T(8,128)(2,1)} %get-tuple-element.208), channel_id=1, source_target_pairs={{0,1},{1,0},{2,3},{3,2},{4,5},{5,4},{6,7},{7,6},{8,9},{9,8},{10,11... | collective-permute-start | bytes 3145736 | tf_op jit(solution)/shard_map/ppermute | solution.py:393
  19.1 49.7 %collective-permute-start = (bf16[2,512,512]{2,1,0:T(8,128)(2,1)}, bf16[2,512,512]{2,1,0:T(8,128)(2,1)}, u32[]{:S(2)}, u32[]{:S(2)}) collective-permute-start(bf16[2,512,512]{2,1,0:T(8,128)(2,1)} %get-tuple-element.209), channel_id=1, source_target_pairs={{0,1},{1,0},{2,3},{3,2},{4,5},{5,4},{6,7},{7,6},{8,9},{9,8},{10,11... | collective-permute-start | bytes 3145736 | tf_op jit(solution)/shard_map/ppermute | solution.py:393
  113.1 94.6 %collective-permute-start.3 = (bf16[2,512,512]{2,1,0:T(8,128)(2,1)S(1)}, bf16[2,512,512]{2,1,0:T(8,128)(2,1)}, u32[]{:S(2)}, u32[]{:S(2)}) collective-permute-start(bf16[2,512,512]{2,1,0:T(8,128)(2,1)S(1)} %get-tuple-element.218), channel_id=1, source_target_pairs={{0,1},{1,0},{2,3},{3,2},{4,5},{5,4},{6,7},{7,6},{8,9},{9,8},{10,11... | collective-permute-start | bytes 3145736 | tf_op jit(solution)/shard_map/ppermute | solution.py:393
  150.7 79.7 %collective-permute-start.1 = (bf16[2,512,512]{2,1,0:T(8,128)(2,1)S(1)}, bf16[2,512,512]{2,1,0:T(8,128)(2,1)}, u32[]{:S(2)}, u32[]{:S(2)}) collective-permute-start(bf16[2,512,512]{2,1,0:T(8,128)(2,1)S(1)} %get-tuple-element.220), channel_id=1, source_target_pairs={{0,1},{1,0},{2,3},{3,2},{4,5},{5,4},{6,7},{7,6},{8,9},{9,8},{10,11... | collective-permute-start | bytes 3145736 | tf_op jit(solution)/shard_map/ppermute | solution.py:393
  228.7 25.5 %collective-permute-start.4 = (bf16[2,512,512]{2,1,0:T(8,128)(2,1)}, bf16[2,512,512]{2,1,0:T(8,128)(2,1)}, u32[]{:S(2)}, u32[]{:S(2)}) collective-permute-start(bf16[2,512,512]{2,1,0:T(8,128)(2,1)} %get-tuple-element.96), channel_id=1, source_target_pairs={{0,1},{1,0},{2,3},{3,2},{4,5},{5,4},{6,7},{7,6},{8,9},{9,8},{10,11... | collective-permute-start | bytes 3145736 | tf_op jit(solution)/shard_map/ppermute | solution.py:393
  230.5 21.1 %copy-start.5 = (bf16[4,512,512]{2,1,0:T(8,128)(2,1)S(1)}, bf16[4,512,512]{2,1,0:T(8,128)(2,1)}, u32[]{:S(2)}) copy-start(bf16[4,512,512]{2,1,0:T(8,128)(2,1)} %get-tuple-element.95) | copy-start | bytes 6291460
  251.2 49.7 %collective-permute-start.5 = (bf16[2,512,512]{2,1,0:T(8,128)(2,1)}, bf16[2,512,512]{2,1,0:T(8,128)(2,1)}, u32[]{:S(2)}, u32[]{:S(2)}) collective-permute-start(bf16[2,512,512]{2,1,0:T(8,128)(2,1)} %get-tuple-element.102), channel_id=1, source_target_pairs={{0,1},{1,0},{2,3},{3,2},{4,5},{5,4},{6,7},{7,6},{8,9},{9,8},{10,11... | collective-permute-start | bytes 3145736 | tf_op jit(solution)/shard_map/ppermute | solution.py:393
  353.5 3.1 copy-start.20
  353.5 4.3 copy-start.15
  353.5 4.3 copy-start.16
  353.5 4.3 copy-start.17
  356.5 154.4 %reduce-scatter.13.cloned.1.call-start = ((), (), s32[]{:S(2)}) async-start(), calls=%async_computation.9 | async-start | bytes 278528
  389.9 2.2 copy-start.2
  392.4 1.6 copy-start.6
  394.1 128.4 %reduce-scatter.7.cloned.1.call-start = ((), (), s32[]{:S(2)}) async-start(), calls=%async_computation.5 | async-start | bytes 147456 | tf_op jit(solution)/shard_map/reduce_scatter | solution.py:509
  454.9 146.9 %reduce-scatter.9.cloned.1.call-start = ((), (), s32[]{:S(2)}) async-start(), calls=%async_computation.6 | async-start | bytes 5013504 | tf_op jit(solution)/shard_map/reduce_scatter | solution.py:508
  458.5 1.6 copy-start.3
  458.6 156.8 %reduce-scatter.11.cloned.1.call-start = ((), (), s32[]{:S(2)}) async-start(), calls=%async_computation.7 | async-start | bytes 442368 | tf_op jit(solution)/shard_map/reduce_scatter | solution.py:509
  460.1 2.7 copy-start.4
  461.3 140.6 %collective-permute-start.6 = (bf16[2,512,512]{2,1,0:T(8,128)(2,1)}, bf16[2,512,512]{2,1,0:T(8,128)(2,1)S(1)}, u32[]{:S(2)}, u32[]{:S(2)}) collective-permute-start(bf16[2,512,512]{2,1,0:T(8,128)(2,1)} %get-tuple-element.212), channel_id=1, source_target_pairs={{0,1},{1,0},{2,3},{3,2},{4,5},{5,4},{6,7},{7,6},{8,9},{9,8},{10,11... | collective-permute-start | bytes 3145736 | tf_op jit(solution)/shard_map/ppermute | solution.py:393
  462.8 53.8 %copy-start.18 = (f32[4,32]{1,0:T(4,128)S(1)}, f32[4,32]{1,0:T(4,128)}, u32[]{:S(2)}) copy-start(f32[4,32]{1,0:T(4,128)} %param.39) | copy-start | bytes 1540
  462.8 53.8 %copy-start.19 = (f32[4,32]{1,0:T(4,128)S(1)}, f32[4,32]{1,0:T(4,128)}, u32[]{:S(2)}) copy-start(f32[4,32]{1,0:T(4,128)} %param.38) | copy-start | bytes 1540
  462.8 60.6 %copy-start.9 = (f32[32,3,256]{2,0,1:T(8,128)S(1)}, f32[32,3,256]{2,0,1:T(8,128)}, u32[]{:S(2)}) copy-start(f32[32,3,256]{2,0,1:T(8,128)} %param.25) | copy-start | bytes 294916
  462.8 60.6 %copy-start.11 = (f32[32,3,256]{2,0,1:T(8,128)S(1)}, f32[32,3,256]{2,0,1:T(8,128)}, u32[]{:S(2)}) copy-start(f32[32,3,256]{2,0,1:T(8,128)} %param.31) | copy-start | bytes 294916
  464.0 137.9 %collective-permute-start.7 = (bf16[2,512,512]{2,1,0:T(8,128)(2,1)}, bf16[2,512,512]{2,1,0:T(8,128)(2,1)}, u32[]{:S(2)}, u32[]{:S(2)}) collective-permute-start(bf16[2,512,512]{2,1,0:T(8,128)(2,1)} %get-tuple-element.214), channel_id=1, source_target_pairs={{0,1},{1,0},{2,3},{3,2},{4,5},{5,4},{6,7},{7,6},{8,9},{9,8},{10,11... | collective-permute-start | bytes 3145736 | tf_op jit(solution)/shard_map/ppermute | solution.py:393
  601.9 14.4 %copy-start.7 = (f32[1024,32]{0,1:T(8,128)S(1)}, f32[1024,32]{0,1:T(8,128)}, u32[]{:S(2)}) copy-start(f32[1024,32]{0,1:T(8,128)} %param.28) | copy-start | bytes 393220
  601.9 16.1 %copy-start.8 = (f32[32,1024]{1,0:T(8,128)S(1)}, f32[32,1024]{1,0:T(8,128)}, u32[]{:S(2)}) copy-start(f32[32,1024]{1,0:T(8,128)} %param.27) | copy-start | bytes 393220
  601.9 18.6 %copy-start.1 = (s32[8,1024]{1,0:T(8,128)S(1)}, s32[8,1024]{1,0:T(8,128)}, u32[]{:S(2)}) copy-start(s32[8,1024]{1,0:T(8,128)} %param.22) | copy-start | bytes 98308
  608.7 11.1 %copy-start.10 = (f32[256,32]{0,1:T(8,128)S(1)}, f32[256,32]{0,1:T(8,128)}, u32[]{:S(2)}) copy-start(f32[256,32]{0,1:T(8,128)} %param.26) | copy-start | bytes 98308
  608.7 11.1 %copy-start.12 = (f32[256,32]{0,1:T(8,128)S(1)}, f32[256,32]{0,1:T(8,128)}, u32[]{:S(2)}) copy-start(f32[256,32]{0,1:T(8,128)} %param.33) | copy-start | bytes 98308
  608.7 11.1 %copy-start.13 = (f32[256,32]{0,1:T(8,128)S(1)}, f32[256,32]{0,1:T(8,128)}, u32[]{:S(2)}) copy-start(f32[256,32]{0,1:T(8,128)} %param.32) | copy-start | bytes 98308
Sparse Core Ops, SparseCore 0:
  11.7 60.0 all-gather.6
  74.7 71.3 all-gather.4
  356.6 96.5 all-reduce.2
  456.6 54.2 reduce-scatter.12
  513.5 9.0 reduce-scatter.6
  526.3 75.5 reduce-scatter.8
  604.2 11.1 reduce-scatter.10
